TPU v7x, 32 devices: a whole 2x2x4 slice. The times are simulated.
32 devices in a mesh: inner: 8 (over y, x, core), outer: 4 (over z).
Axes of the slice: x: 2, y: 2, z: 4, core: 2. Of those that a mesh axis runs over, the one named last changes fastest.
Arguments:
- embedding: bfloat16 [98304, 4096], P(('inner', 'outer')), may hold values from -80 to 80
- test_matrix: bfloat16 [4096, 256], replicated, may hold values from -0.09375 to 0.09375
Outputs:
- projection: float32 [4096, 256], P(('inner', 'outer'))
All inputs are finite; a program needn't handle non-finite values.
Results may differ from a plain program's by a relative error of at most 0.00035.
Values sent between devices are 32-bit elements; how exact they have to be, the bound alone decides.
A program may use at most 128 MiB of HBM per device.

v0:
```python
import jax
import jax.numpy as jnp
from jax import lax
from jax.sharding import PartitionSpec as P


def local(embedding, test_matrix):
    sketch = jnp.dot(embedding, test_matrix, preferred_element_type=jnp.float32)
    local_gram = jnp.dot(
        sketch.T, sketch, precision=lax.Precision.HIGHEST, preferred_element_type=jnp.float32
    )
    partial_gram = lax.psum(local_gram, "inner")
    gram = lax.psum(partial_gram, "outer")
    lower = jnp.linalg.cholesky(gram)
    basis = lax.linalg.triangular_solve(
        lower, sketch, left_side=False, lower=True, transpose_a=True
    ).astype(jnp.bfloat16)
    sectioned = lax.psum_scatter(
        lax.dot_general(
            embedding, basis, (((0,), (0,)), ((), ())), preferred_element_type=jnp.float32
        ),
        "inner",
        scatter_dimension=0,
        tiled=True,
    )
    projection = lax.psum_scatter(sectioned, "outer", scatter_dimension=0, tiled=True)
    return projection


def solution(mesh):
    return jax.shard_map(
        local,
        mesh=mesh,
        in_specs=(P(("inner", "outer"), None), P()),
        out_specs=P(("inner", "outer"), None),
        check_vma=False,
    )
```

profile of v0, /device:TPU:0, one launch (start us, length us, event | category | flops | bytes accessed | tf_op | source)
XLA Modules:
  0.0 286.8 jit_solution(179800366662152361)
XLA Ops:
  6.5 1.6 copy-done
  8.1 11.8 %fusion.13 = f32[3072,256]{1,0:T(8,128)S(1)} fusion(bf16[3072,4096]{1,0:T(8,128)(2,1)} %param.2, bf16[4096,256]{1,0:T(8,128)(2,1)S(1)} %copy-done), kind=kOutput, calls=%fused_computation.34 | convolution fusion | flops 6442450944 | bytes 30408704 | tf_op jit(solution)/shard_map/dot_general | solution.py:8
  20.0 1.7 copy-done.1
  21.6 6.1 %fusion.14 = f32[256,256]{0,1:T(8,128)} fusion(f32[3072,256]{1,0:T(8,128)S(1)} %fusion.13), kind=kOutput, calls=%fused_computation.35 | convolution fusion | flops 2415919104 | bytes 3407872 | tf_op jit(solution)/shard_map/dot_general | solution.py:9
  27.8 56.3 %all-reduce.4.cloned.1.call-done = f32[256,256]{0,1:T(8,128)} async-done(((f32[256,256]{0,1:T(8,128)}), f32[256,256]{0,1:T(8,128)}) %all-reduce.4.cloned.1.call-update) | async-done | bytes 262160 | tf_op jit(solution)/shard_map/psum | solution.py:12
  84.3 36.9 %all-reduce.6.cloned.1.call-done = f32[256,256]{0,1:T(8,128)} async-done(((f32[256,256]{0,1:T(8,128)}), f32[256,256]{0,1:T(8,128)}) %all-reduce.6.cloned.1.call-update) | async-done | bytes 262160 | tf_op jit(solution)/shard_map/psum | solution.py:13
  121.2 1.1 copy.4
  122.3 1.0 fusion.5
  123.3 11.7 %cholesky.50 = f32[128,128]{1,0:T(8,128)S(1)} custom-call(f32[128,128]{1,0:T(8,128)S(1)} %cholesky.118), custom_call_target="Cholesky" | custom-call | tf_op jit(solution)/shard_map/jit(cholesky)/cholesky | solution.py:14
  135.1 9.8 %custom-call.14 = f32[1,128,128]{1,2,0:T(8,128)S(1)} custom-call(f32[1,128,128]{2,1,0:T(8,128)S(1)} %get-tuple-element.26), custom_call_target="InvertDiagBlocksLowerTriangular" | custom-call | tf_op jit(solution)/shard_map/jit(cholesky)/cholesky | solution.py:14
  145.4 11.7 %cholesky.105 = f32[128,128]{1,0:T(8,128)S(1)} custom-call(f32[128,128]{1,0:T(8,128)S(1)} %convolution_subtract_fusion.1), custom_call_target="Cholesky" | custom-call | tf_op jit(solution)/shard_map/jit(cholesky)/cholesky | solution.py:14
  157.1 0.7 compare_reduce_fusion
  159.1 3.8 %while.1 = (s32[]{:T(128)}, f32[256,256]{1,0:T(8,128)S(1)}, s32[2,2]{1,0:T(2,128)S(1)}, f32[2,128,128]{2,1,0:T(8,128)S(1)}, s32[]{:T(128)}) while((s32[]{:T(128)}, f32[256,256]{1,0:T(8,128)S(1)}, s32[2,2]{1,0:T(2,128)S(1)}, f32[2,128,128]{2,1,0:T(8,128)S(1)}, s32[]{:T(128)}) %tuple.24), condition=%wide.while_cond, body=%wide.while_body.sunk | while | flops 2 | bytes 131189 | solution.py:15
  159.8 1.3 bitcast_dynamic-update-slice_fusion.2
  161.1 0.6 fusion.25
  161.7 1.3 bitcast_dynamic-update-slice_fusion.2
  162.9 19.7 %custom-call.15 = f32[2,128,128]{1,2,0:T(8,128)S(1)} custom-call(f32[2,128,128]{2,1,0:T(8,128)S(1)} %get-tuple-element.12), custom_call_target="InvertDiagBlocksLowerTriangular" | custom-call | tf_op jit(solution)/shard_map/triangular_solve | solution.py:15
  182.6 3.1 %fusion.12 = (bf16[3072,128]{0,1:T(8,128)(2,1)S(1)}, f32[3072,128]{0,1:T(8,128)S(1)}) fusion(f32[2,128,128]{1,2,0:T(8,128)S(1)} %custom-call.15, f32[3072,256]{1,0:T(8,128)} %copy-done.1), kind=kOutput, calls=%fused_computation.33 | convolution fusion | flops 604372992 | bytes 3997696 | tf_op jit(solution)/shard_map/triangular_solve | solution.py:15
  185.7 2.6 convolution_subtract_fusion
  188.4 1.5 convolution_convert_fusion
  189.9 13.5 %convolution_bitcast_fusion = f32[4096,256]{0,1:T(8,128)} fusion(bf16[3072,4096]{1,0:T(8,128)(2,1)} %param.2, bf16[3072,128]{0,1:T(8,128)(2,1)S(1)} %convolution_convert_fusion, bf16[3072,128]{0,1:T(8,128)(2,1)S(1)} %get-tuple-element.29), kind=kOutput, calls=%fused_computation.2 | convolution fusion | flops 6445596672 | bytes 30932992 | tf_op jit(solution)/shard_map/dot_general | solution.py:19
  203.5 51.2 %reduce-scatter.3.cloned.1.call-done = f32[512,256]{0,1:T(8,128)} async-done(((f32[4096,256]{0,1:T(8,128)}), f32[512,256]{0,1:T(8,128)}) %reduce-scatter.3.cloned.1.call-update) | async-done | bytes 524304 | tf_op jit(solution)/shard_map/reduce_scatter | solution.py:18
  254.7 23.9 %reduce-scatter.5.cloned.1.call-done = f32[128,256]{0,1:T(8,128)} async-done(((f32[512,256]{0,1:T(8,128)}), f32[128,256]{0,1:T(8,128)}) %reduce-scatter.5.cloned.1.call-update) | async-done | bytes 131088 | tf_op jit(solution)/shard_map/reduce_scatter | solution.py:26
  278.6 1.7 copy.5
  (25 shorter events, 1.6 us)
Async XLA Ops:
  6.5 1.6 copy-start
  6.5 77.5 %all-reduce.4.cloned.1.call-start = ((), (), s32[]{:S(2)}) async-start(), calls=%async_computation.2 | async-start | bytes 524288 | tf_op jit(solution)/shard_map/psum | solution.py:12
  20.0 1.7 copy-start.1
  27.7 93.5 %all-reduce.6.cloned.1.call-start = ((), (), s32[]{:S(2)}) async-start(), calls=%async_computation.3 | async-start | bytes 524288 | tf_op jit(solution)/shard_map/psum | solution.py:13
  84.1 170.6 %reduce-scatter.3.cloned.1.call-start = ((), (), s32[]{:S(2)}) async-start(), calls=%async_computation.4 | async-start | bytes 4718592 | tf_op jit(solution)/shard_map/reduce_scatter | solution.py:18
  182.6 3.1 %copy-start.2 = (f32[3072,256]{1,0:T(8,128)S(1)}, f32[3072,256]{1,0:T(8,128)}, u32[]{:S(2)}) copy-start(f32[3072,256]{1,0:T(8,128)} %copy-done.1) | copy-start | bytes 9437188
  203.5 75.1 %reduce-scatter.5.cloned.1.call-start = ((), (), s32[]{:S(2)}) async-start(), calls=%async_computation.5 | async-start | bytes 655360 | tf_op jit(solution)/shard_map/reduce_scatter | solution.py:26
Sparse Core Ops, SparseCore 0:
  27.8 56.1 all-reduce.3
  86.5 34.6 all-reduce.5
  203.6 51.0 reduce-scatter.2
  256.9 21.6 reduce-scatter.4
where the time goes:
time: 287 us
  waiting for transfers between devices  168 us (59%)
  other arithmetic  54.7 us (19%)
  matrix products  39.2 us (14%)
  between operations  14.4 us (5%)
  local copies, waits for them, and re-layouts  9.71 us (3%)
    psum x1, waiting for transfers between devices, local(): partial_gram = lax.psum(local_gram, 'inner')  56.3 us
    reduce_scatter x1, waiting for transfers between devices, local(): lax.psum_scatter(lax.dot_general(embedding, basis, (((0,), (0,)), ((), ()...  51.2 us
    psum x1, waiting for transfers between devices, local(): gram = lax.psum(partial_gram, 'outer')  36.9 us
    another operation x6, other arithmetic, local(): lower = jnp.linalg.cholesky(gram)  34 us
    reduce_scatter x1, waiting for transfers between devices, local(): lax.psum_scatter(sectioned, 'outer', scatter_dimension=0, tiled=True)  23.9 us
    another operation x3, other arithmetic, local(): lax.linalg.triangular_solve(lower, sketch, left_side=False, lower=True, t...  19.7 us
    dot_general x1, matrix products, local(): lax.dot_general(embedding, basis, (((0,), (0,)), ((), ())), preferred_ele...  13.5 us
    dot_general x1, matrix products, local(): sketch = jnp.dot(embedding, test_matrix, preferred_element_type=jnp.float32)  11.8 us
  transfers between devices with their start and end apart: 4, of which 4 were waited for; matrix products, arithmetic and copies ran while one was open for 0% of the time, Pallas kernels for 0%

commit v1 on v0

v1 whole, which is shorter than its diff:
```python
import functools

import jax
import jax.numpy as jnp
from jax import lax
from jax.experimental import pallas as pl
from jax.experimental.pallas import tpu as pltpu
from jax.sharding import PartitionSpec as P

MESH = pl.DeviceIdType.MESH
HIGHEST = lax.Precision.HIGHEST
VMEM_LIMIT = 56 * 1024 * 1024


def dot(a, b, precision=None):
    return jnp.dot(a, b, precision=precision, preferred_element_type=jnp.float32)


def gram_kernel(
    n_in, n_out, steps, e_ref, t_ref, st_ref, g_ref,
    acc, whole, recv1, recv2, s1, r1, s2, r2, s3, r3,
):
    step = pl.program_id(0)
    me_in, me_out = lax.axis_index("inner"), lax.axis_index("outer")
    rows = acc.shape[0] // n_in
    barrier = pltpu.get_barrier_semaphore()
    in_peers = [lax.rem(me_in + d, n_in) for d in range(n_in)]
    out_peers = [lax.rem(me_out + d, n_out) for d in range(n_out)]

    @pl.when(step == 0)
    def _():
        for d in range(1, n_in):
            pl.semaphore_signal(barrier, inc=1, device_id=(in_peers[d], me_out), device_id_type=MESH)
        for d in range(1, n_out):
            pl.semaphore_signal(barrier, inc=1, device_id=(me_in, out_peers[d]), device_id_type=MESH)
        acc[...] = jnp.zeros_like(acc)

    s = dot(e_ref[...], t_ref[...])
    st = s.T
    st_ref[...] = st
    acc[...] += dot(st, s, HIGHEST)

    @pl.when(step == steps - 1)
    def _():
        pl.semaphore_wait(barrier, n_in + n_out - 2)
        copies = []
        for d in range(1, n_in):
            peer = in_peers[d]
            copies.append(pltpu.make_async_remote_copy(
                src_ref=acc.at[pl.ds(pl.multiple_of(peer * rows, rows), rows), :],
                dst_ref=recv1.at[d],
                send_sem=s1.at[d], recv_sem=r1.at[d],
                device_id=(peer, me_out), device_id_type=MESH,
            ))
            copies[-1].start()
        total = acc[pl.ds(pl.multiple_of(me_in * rows, rows), rows), :]
        for d in range(1, n_in):
            copies[d - 1].wait_recv()
            total += recv1[d]
        recv2[me_out] = total
        seconds = []
        for d in range(1, n_out):
            seconds.append(pltpu.make_async_remote_copy(
                src_ref=recv2.at[me_out],
                dst_ref=recv2.at[me_out],
                send_sem=s2.at[d], recv_sem=r2.at[d],
                device_id=(me_in, out_peers[d]), device_id_type=MESH,
            ))
            seconds[-1].start()
        for c in copies:
            c.wait_send()
        for c in seconds:
            c.wait_recv()
        total = recv2[0]
        for d in range(1, n_out):
            total += recv2[d]
        mine = pl.ds(pl.multiple_of(me_in * rows, rows), rows)
        whole[mine, :] = total
        thirds = []
        for d in range(1, n_in):
            thirds.append(pltpu.make_async_remote_copy(
                src_ref=whole.at[mine, :],
                dst_ref=whole.at[mine, :],
                send_sem=s3.at[d], recv_sem=r3.at[d],
                device_id=(in_peers[d], me_out), device_id_type=MESH,
            ))
            thirds[-1].start()
        for c in seconds:
            c.wait_send()
        for c in thirds:
            c.wait()
        g_ref[...] = whole[...]


def sketch_and_gram(embedding, test_matrix, n_in, n_out):
    rows, width = embedding.shape
    rank = test_matrix.shape[1]
    chunk = 256
    steps = rows // chunk
    part = rank // n_in
    dma = pltpu.SemaphoreType.DMA
    return pl.pallas_call(
        functools.partial(gram_kernel, n_in, n_out, steps),
        grid=(steps,),
        out_shape=(
            jax.ShapeDtypeStruct((rank, rows), jnp.float32),
            jax.ShapeDtypeStruct((rank, rank), jnp.float32),
        ),
        in_specs=[
            pl.BlockSpec((chunk, width), lambda i: (i, 0)),
            pl.BlockSpec((width, rank), lambda i: (0, 0)),
        ],
        out_specs=(
            pl.BlockSpec((rank, chunk), lambda i: (0, i)),
            pl.BlockSpec(memory_space=pltpu.VMEM),
        ),
        scratch_shapes=[
            pltpu.VMEM((rank, rank), jnp.float32),
            pltpu.VMEM((rank, rank), jnp.float32),
            pltpu.VMEM((n_in, part, rank), jnp.float32),
            pltpu.VMEM((n_out, part, rank), jnp.float32),
            dma((n_in,)), dma((n_in,)), dma((n_out,)), dma((n_out,)), dma((n_in,)), dma((n_in,)),
        ],
        compiler_params=pltpu.CompilerParams(
            collective_id=0, has_side_effects=True, vmem_limit_bytes=VMEM_LIMIT,
        ),
        cost_estimate=pl.CostEstimate(
            flops=2 * rows * width * rank, bytes_accessed=rows * width * 2, transcendentals=0
        ),
    )(embedding, test_matrix)


def sweep(src, dst):
    n = src.shape[0]
    groups = n // 8
    lane = lax.broadcasted_iota(jnp.int32, (8, n), 1)
    sub = lax.broadcasted_iota(jnp.int32, (8, n), 0)
    full = (8, n)
    t = [src[8 * i : 8 * i + 8, :] for i in range(groups)]
    for g in range(groups):
        base = 8 * g
        panel = (lane >= base) & (lane < base + 8)
        cols = [jnp.broadcast_to(t[g][:, base + k : base + k + 1], full) for k in range(8)]
        top = jnp.where(panel, 0.0, t[g])
        scaled, splats, pivots = [], [], None
        for k in range(8):
            pivot = jnp.broadcast_to(cols[k][k : k + 1, :], full)
            inv = 1.0 / pivot
            row = jnp.broadcast_to(top[k : k + 1, :], full)
            scaled.append(jnp.where(lane == base + k, inv, row * inv))
            splat = {l: jnp.broadcast_to(cols[l][k : k + 1, :], full) * inv for l in range(k + 1, 8)}
            splats.append(splat)
            pivots = pivot if k == 0 else jnp.where(sub >= k, pivot, pivots)
            if k < 7:
                below = jnp.where(sub > k, cols[k], 0.0)
                for l in range(k + 1, 8):
                    cols[l] = cols[l] - below * splat[l]
                top = top - below * scaled[k]
        rows = jnp.where(lane == base + sub, 1.0, jnp.where(lane < base + 8, top, 0.0))
        dst[base : base + 8, :] = rows / jnp.sqrt(pivots)
        for i in range(g + 1, groups):
            c = [jnp.broadcast_to(t[i][:, base + k : base + k + 1], full) for k in range(8)]
            x = jnp.where(panel, 0.0, t[i])
            for k in range(8):
                for l in range(k + 1, 8):
                    c[l] = c[l] - c[k] * splats[k][l]
                x = x - c[k] * scaled[k]
            t[i] = x


def factor_kernel(g_ref, m_ref, a, m, x):
    half = a.shape[0]
    step = pl.program_id(0)

    @pl.when(step == 0)
    def _():
        a[...] = g_ref[:half, :half]

    @pl.when(step == 1)
    def _():
        x[...] = dot(m[...], g_ref[:half, half:], HIGHEST)
        a[...] = g_ref[half:, half:] - dot(x[...].T, x[...], HIGHEST)

    @pl.when(step == 1)
    def _():
        m_ref[:half, :half] = m[...]
        m_ref[:half, half:] = jnp.zeros_like(m)

    sweep(a, m)

    @pl.when(step == 1)
    def _():
        m_ref[half:, half:] = m[...]
        y = dot(x[...].T, m_ref[:half, :half], HIGHEST)
        m_ref[half:, :half] = -dot(m[...], y, HIGHEST)


def inverse_factor(gram):
    n = gram.shape[0]
    half = n // 2
    block = pltpu.VMEM((half, half), jnp.float32)
    return pl.pallas_call(
        factor_kernel,
        grid=(2,),
        out_shape=jax.ShapeDtypeStruct((n, n), jnp.float32),
        in_specs=[pl.BlockSpec(memory_space=pltpu.VMEM)],
        out_specs=pl.BlockSpec(memory_space=pltpu.VMEM),
        scratch_shapes=[block, block, block],
    )(gram)


def project_kernel(
    n_in, n_out, m_ref, st_ref, e_ref, out_ref,
    ebuf, basis, part, recv1, *rest,
):
    bits = n_in.bit_length() - 1
    rounds = bits - 1
    recv_a, recv_b = rest[:rounds], rest[rounds : 2 * rounds]
    last, esem, s1, r1, sa, ra, sb, rb, sz, rz = rest[2 * rounds :]
    me_in, me_out = lax.axis_index("inner"), lax.axis_index("outer")
    width = ebuf.shape[2]
    rank = basis.shape[0]
    half = rank // 2

    def flipped(r):
        index = me_in
        for b in range(bits):
            if r >> b & 1:
                bit = lax.rem(me_in // (1 << b), 2)
                index = index + (1 - 2 * bit) * (1 << b)
        return index

    peers = [flipped(1 << b) for b in range(bits)]
    out_peers = [lax.rem(me_out + d, n_out) for d in range(n_out)]
    barrier = pltpu.get_barrier_semaphore()
    for p in peers:
        pl.semaphore_signal(barrier, inc=1, device_id=(p, me_out), device_id_type=MESH)
    for d in range(1, n_out):
        pl.semaphore_signal(barrier, inc=1, device_id=(me_in, out_peers[d]), device_id_type=MESH)

    order = sorted(range(n_in // 2), key=lambda r: (-bin(r).count("1"), r))
    sequence = [2 * r + 1 for r in order] + [2 * r for r in order]
    loads = {}
    for r in sequence:
        start = pl.multiple_of(flipped(r) * width, width)
        loads[r] = pltpu.make_async_copy(e_ref.at[:, pl.ds(start, width)], ebuf.at[r], esem.at[r])
        loads[r].start()

    rows = basis.shape[1]
    for c in range(0, rows, 512):
        basis[:, c : c + 512] = dot(m_ref[...], st_ref[:, c : c + 512], HIGHEST).astype(jnp.bfloat16)

    pl.semaphore_wait(barrier, bits + n_out - 1)

    def remote(src, dst, send, recv, device):
        copy = pltpu.make_async_remote_copy(
            src_ref=src, dst_ref=dst, send_sem=send, recv_sem=recv,
            device_id=device, device_id_type=MESH,
        )
        copy.start()
        return copy

    sent = []
    first = {}
    for r in order:
        loads[2 * r + 1].wait()
        part[r] = dot(basis[...], ebuf[2 * r + 1]).T
        first[r] = remote(part.at[r], recv1.at[r], s1.at[r], r1.at[r], (peers[0], me_out))
        sent.append(first[r])

    lanes = {"a": pl.ds(0, half), "b": pl.ds(half, half)}
    way = {"a": list(range(1, bits)), "b": list(range(bits - 1, 0, -1))}
    bufs = {"a": recv_a, "b": recv_b}
    sems = {"a": (sa, ra), "b": (sb, rb)}
    pending = {}
    count = {"a": 0, "b": 0}

    def squeeze(index, remaining, b):
        at = remaining.index(b)
        return (index >> (at + 1) << at) | (index & ((1 << at) - 1))

    def send_chunk(which, stage, index, src):
        remaining = sorted(way[which][stage:])
        b = way[which][stage]
        at = remaining.index(b)
        target = squeeze(index, remaining, b)
        if index >> at & 1:
            k = count[which]
            count[which] += 1
            send, recv = sems[which]
            pending[which, stage, target] = remote(
                src, bufs[which][stage].at[target], send.at[k], recv.at[k], (peers[b], me_out)
            )
            sent.append(pending[which, stage, target])

    for r in order:
        loads[2 * r].wait()
        own = dot(basis[...], ebuf[2 * r]).T
        first[r].wait_recv()
        recv1[r] = recv1[r] + own
        for which in ("a", "b"):
            send_chunk(which, 0, r, recv1.at[r, :, lanes[which]])

    for stage in range(rounds):
        for which in ("a", "b"):
            remaining = sorted(way[which][stage:])
            b = way[which][stage]
            at = remaining.index(b)
            slots = sorted(range(1 << (len(remaining) - 1)), key=lambda v: (-bin(v).count("1"), v))
            for target in slots:
                index = (target >> at << (at + 1)) | (target & ((1 << at) - 1))
                pending[which, stage, target].wait_recv()
                buf = bufs[which][stage]
                if stage == 0:
                    kept = recv1[index, :, lanes[which]]
                else:
                    kept = bufs[which][stage - 1][index]
                buf[target] = buf[target] + kept
                if stage + 1 < rounds:
                    send_chunk(which, stage + 1, target, buf.at[target])

    block = out_ref.shape[0]
    finals = []
    for d in range(1, n_out):
        theirs = pl.ds(pl.multiple_of(out_peers[d] * block, block), block)
        for w, which in enumerate(("a", "b")):
            finals.append(remote(
                bufs[which][-1].at[0, theirs, :], last.at[me_out, :, lanes[which]],
                sz.at[w, d], rz.at[w, d], (me_in, out_peers[d]),
            ))
    mine = pl.ds(pl.multiple_of(me_out * block, block), block)
    for which in ("a", "b"):
        last[me_out, :, lanes[which]] = bufs[which][-1][0, mine, :]
    for c in finals:
        c.wait_recv()
    total = last[0]
    for d in range(1, n_out):
        total = total + last[d]
    out_ref[...] = total
    for c in sent + finals:
        c.wait_send()


def project(inverse, sketch_t, embedding, n_in, n_out):
    rows, width = embedding.shape
    rank = inverse.shape[0]
    block = width // n_in
    bits = n_in.bit_length() - 1
    rounds = bits - 1
    dma = pltpu.SemaphoreType.DMA
    f32 = jnp.float32
    halves = [pltpu.VMEM((n_in >> (s + 2), block, rank // 2), f32) for s in range(rounds)]
    vmem = pl.BlockSpec(memory_space=pltpu.VMEM)
    return pl.pallas_call(
        functools.partial(project_kernel, n_in, n_out),
        out_shape=jax.ShapeDtypeStruct((block // n_out, rank), f32),
        in_specs=[vmem, vmem, pl.BlockSpec(memory_space=pl.ANY)],
        out_specs=vmem,
        scratch_shapes=[
            pltpu.VMEM((n_in, rows, block), jnp.bfloat16),
            pltpu.VMEM((rank, rows), jnp.bfloat16),
            pltpu.VMEM((n_in // 2, block, rank), f32),
            pltpu.VMEM((n_in // 2, block, rank), f32),
            *halves,
            *halves,
            pltpu.VMEM((n_out, block // n_out, rank), f32),
            dma((n_in,)),
            dma((n_in // 2,)), dma((n_in // 2,)),
            dma((n_in // 2,)), dma((n_in // 2,)),
            dma((n_in // 2,)), dma((n_in // 2,)),
            dma((2, n_out)), dma((2, n_out)),
        ],
        compiler_params=pltpu.CompilerParams(
            collective_id=1, has_side_effects=True, vmem_limit_bytes=VMEM_LIMIT,
        ),
        cost_estimate=pl.CostEstimate(
            flops=2 * rows * width * rank, bytes_accessed=rows * width * 2, transcendentals=0
        ),
    )(inverse, sketch_t, embedding)


def local(n_in, n_out, embedding, test_matrix):
    sketch_t, gram = sketch_and_gram(embedding, test_matrix, n_in, n_out)
    inverse = inverse_factor(gram)
    return project(inverse, sketch_t, embedding, n_in, n_out)


def solution(mesh):
    n_in, n_out = mesh.shape["inner"], mesh.shape["outer"]
    return jax.shard_map(
        functools.partial(local, n_in, n_out),
        mesh=mesh,
        in_specs=(P(("inner", "outer"), None), P()),
        out_specs=P(("inner", "outer"), None),
        check_vma=False,
    )
```

time: 287 us -> 94.1 us (0.33)
  waiting for transfers between devices: 168 us -> 0 us
  Pallas kernels: 0 us -> 91.9 us
  other arithmetic: 54.7 us -> 0 us
  matrix products: 39.2 us -> 0 us
  between operations: 14.4 us -> 0.02 us
  local copies, waits for them, and re-layouts: 9.71 us -> 1.57 us
    psum x2 -> x0, waiting for transfers between devices: 93.2 us -> none  [the longest x1 56.3 us: local(): partial_gram = lax.psum(local_gram, 'inner')]
    pallas_call x0 -> x3, Pallas kernels: none -> 91.9 us  [the longest x1 43 us: project(): pl.pallas_call(functools.partial(project_kernel, n_in, n_out), out_shape=...]
    reduce_scatter x2 -> x0, waiting for transfers between devices: 75 us -> none  [the longest x1 51.2 us: local(): lax.psum_scatter(lax.dot_general(embedding, basis, (((0,), (0,)), ((), ()...]
    another operation x9 -> x0, other arithmetic: 53.7 us -> none  [the longest x6 34 us: local(): lower = jnp.linalg.cholesky(gram)]
    dot_general x3 -> x0, matrix products: 31.4 us -> none  [the longest x1 13.5 us: local(): lax.dot_general(embedding, basis, (((0,), (0,)), ((), ())), preferred_ele...]
    another operation x5 -> x0, matrix products: 7.75 us -> none  [the longest x3 7.27 us: local(): lax.linalg.triangular_solve(lower, sketch, left_side=False, lower=True, t...]
    another operation x9 -> x0, local copies, waits for them, and re-layouts: 3.72 us -> none
  transfers between devices with their start and end apart: 4 -> 0, of which waited for: 4 -> 0; matrix products, arithmetic and copies ran while one was open for 0% -> 0% of each run, Pallas kernels for 0% -> 0%
where the time goes in v1:
time: 94.1 us; the launch traced here: 93.5 us
  Pallas kernels  91.9 us (98%)
  local copies, waits for them, and re-layouts  1.57 us (2%)
    pallas_call x1, Pallas kernels, project(): pl.pallas_call(functools.partial(project_kernel, n_in, n_out), out_shape=...  43 us
    pallas_call x1, Pallas kernels, sketch_and_gram(): pl.pallas_call(functools.partial(gram_kernel, n_in, n_out, steps), grid=(...  38.4 us
    pallas_call x1, Pallas kernels, inverse_factor(): pl.pallas_call(factor_kernel, grid=(2,), out_shape=jax.ShapeDtypeStruct((...  10.4 us

profile of v1, /device:TPU:0, one launch (start us, length us, event | category | flops | bytes accessed | tf_op | source)
XLA Modules:
  0.0 93.5 jit_solution(16646335120457901158)
XLA Ops:
  0.0 38.4 %shard_map.28 = (f32[256,3072]{1,0:T(8,128)}, f32[256,256]{1,0:T(8,128)}) custom-call(bf16[3072,4096]{1,0:T(8,128)(2,1)} %e_ref.3, bf16[4096,256]{1,0:T(8,128)(2,1)} %t_ref.1), custom_call_target="tpu_custom_call" | custom-call | flops 6442450944 | bytes 25165824 | tf_op jit(solution)/shard_map/pallas_call | solution.py:102
  38.4 10.4 %shard_map.29.m_ref = f32[256,256]{1,0:T(8,128)} custom-call(f32[256,256]{1,0:T(8,128)} %get-tuple-element.7.g_ref), custom_call_target="tpu_custom_call" | custom-call | tf_op jit(solution)/shard_map/pallas_call | solution.py:202
  48.9 43.0 %shard_map.30 = f32[128,256]{1,0:T(8,128)} custom-call(f32[256,256]{1,0:T(8,128)} %shard_map.29.m_ref, f32[256,3072]{1,0:T(8,128)} %get-tuple-element.8.st_ref, bf16[3072,4096]{1,0:T(8,128)(2,1)} %e_ref.3), custom_call_target="tpu_custom_call" | custom-call | flops 6442450944 | bytes 25165824 | tf_op jit(solution)/shard_map/pallas_call | solution.py:354
  91.9 1.6 %copy.4 = f32[128,256]{1,0:T(8,128)} copy(f32[128,256]{1,0:T(8,128)} %shard_map.30) | data formatting | bytes 262144

commit v2 on v0

v2 whole, which is shorter than its diff:
```python
import functools

import jax
import jax.numpy as jnp
from jax import lax
from jax.experimental import pallas as pl
from jax.experimental.pallas import tpu as pltpu
from jax.sharding import PartitionSpec as P

MESH = pl.DeviceIdType.MESH
HIGHEST = lax.Precision.HIGHEST
VMEM_LIMIT = 58 * 1024 * 1024
CHUNK = 384


def dot(a, b, precision=None):
    return jnp.dot(a, b, precision=precision, preferred_element_type=jnp.float32)


def remote(src, dst, send, recv, device):
    copy = pltpu.make_async_remote_copy(
        src_ref=src, dst_ref=dst, send_sem=send, recv_sem=recv,
        device_id=device, device_id_type=MESH,
    )
    copy.start()
    return copy


def sweep(a, store):
    n = a.shape[0]
    groups = n // 8
    lane = lax.broadcasted_iota(jnp.int32, (8, n), 1)
    sub = lax.broadcasted_iota(jnp.int32, (8, n), 0)
    full = (8, n)
    t = [a[8 * i : 8 * i + 8, :] for i in range(groups)]
    for g in range(groups):
        base = 8 * g
        panel = (lane >= base) & (lane < base + 8)
        cols = [jnp.broadcast_to(t[g][:, base + k : base + k + 1], full) for k in range(8)]
        top = jnp.where(panel, 0.0, t[g])
        scaled, splats, pivots = [], [], None
        for k in range(8):
            pivot = jnp.broadcast_to(cols[k][k : k + 1, :], full)
            inv = 1.0 / pivot
            row = jnp.broadcast_to(top[k : k + 1, :], full)
            scaled.append(jnp.where(lane == base + k, inv, row * inv))
            splat = {l: jnp.broadcast_to(cols[l][k : k + 1, :], full) * inv for l in range(k + 1, 8)}
            splats.append(splat)
            pivots = pivot if k == 0 else jnp.where(sub >= k, pivot, pivots)
            if k < 7:
                below = jnp.where(sub > k, cols[k], 0.0)
                for l in range(k + 1, 8):
                    cols[l] = cols[l] - below * splat[l]
                top = top - below * scaled[k]
        rows = jnp.where(lane == base + sub, 1.0, jnp.where(lane < base + 8, top, 0.0))
        store(base, rows / jnp.sqrt(pivots))
        for first in range(g + 1, groups, 4):
            those = range(first, min(first + 4, groups))
            old = jnp.stack([t[i] for i in those])
            c = [jnp.broadcast_to(old[:, :, base + k : base + k + 1], old.shape) for k in range(8)]
            x = jnp.where(panel, 0.0, old)
            for k in range(8):
                for l in range(k + 1, 8):
                    c[l] = c[l] - c[k] * splats[k][l]
                x = x - c[k] * scaled[k]
            for at, i in enumerate(those):
                t[i] = x[at]


def kernel(
    n_in, n_out, e_ref, t_ref, out_ref,
    ebuf, tbuf, s_last, st, basis, acc, whole, recv1, recv2, m,
    part, first, stages, final, last,
    esem, tsem, s1, r1, s2, r2, s3, r3, sc, rc, sw, rw, sz, rz,
):
    me_in, me_out = lax.axis_index("inner"), lax.axis_index("outer")
    rows, width = ebuf.shape
    rank = acc.shape[0]
    half = rank // 2
    bits = n_in.bit_length() - 1
    rounds = bits - 1
    block = width // n_in
    out_block = block // n_out
    steps = rows // CHUNK

    barrier = pltpu.get_barrier_semaphore()
    in_peers = [lax.rem(me_in + d, n_in) for d in range(n_in)]
    out_peers = [lax.rem(me_out + d, n_out) for d in range(n_out)]
    for d in range(1, n_in):
        pl.semaphore_signal(barrier, inc=1, device_id=(in_peers[d], me_out), device_id_type=MESH)
    for d in range(1, n_out):
        pl.semaphore_signal(barrier, inc=1, device_id=(me_in, out_peers[d]), device_id_type=MESH)

    test_copy = pltpu.make_async_copy(t_ref, tbuf, tsem)
    test_copy.start()

    def load(i):
        span = pl.ds(pl.multiple_of(i * CHUNK, CHUNK), CHUNK)
        return pltpu.make_async_copy(e_ref.at[span, :], ebuf.at[span, :], esem.at[i])

    for i in range(steps):
        load(i).start()

    def sketch(i):
        span = pl.ds(pl.multiple_of(i * CHUNK, CHUNK), CHUNK)
        return dot(ebuf[span, :], tbuf[...])

    def keep(i, s):
        span = pl.ds(pl.multiple_of(i * CHUNK, CHUNK), CHUNK)
        s_last[...] = s
        st[:, span] = s.T

    def gram_term(i):
        span = pl.ds(pl.multiple_of(i * CHUNK, CHUNK), CHUNK)
        return dot(st[:, span], s_last[...], HIGHEST)

    test_copy.wait()
    load(0).wait()
    keep(0, sketch(0))
    acc[...] = jnp.zeros_like(acc)

    def body(i, carry):
        load(i).wait()
        s = sketch(i)
        acc[...] += gram_term(i - 1)
        keep(i, s)
        return carry

    lax.fori_loop(1, steps, body, 0)
    acc[...] += gram_term(steps - 1)

    share = rank // n_in
    pl.semaphore_wait(barrier, n_in + n_out - 2)
    mine = pl.ds(pl.multiple_of(me_in * share, share), share)
    sent = []
    copies = []
    for d in range(1, n_in):
        theirs = pl.ds(pl.multiple_of(in_peers[d] * share, share), share)
        copies.append(remote(acc.at[theirs, :], recv1.at[d], s1.at[d], r1.at[d], (in_peers[d], me_out)))
    sent += copies
    total = acc[mine, :]
    for d in range(1, n_in):
        copies[d - 1].wait_recv()
        total = total + recv1[d]
    recv2[me_out] = total
    copies = []
    for d in range(1, n_out):
        copies.append(remote(recv2.at[me_out], recv2.at[me_out], s2.at[d], r2.at[d], (me_in, out_peers[d])))
    sent += copies
    for c in copies:
        c.wait_recv()
    total = recv2[0]
    for d in range(1, n_out):
        total = total + recv2[d]
    whole[mine, :] = total
    copies = []
    for d in range(1, n_in):
        copies.append(remote(whole.at[mine, :], whole.at[mine, :], s3.at[d], r3.at[d], (in_peers[d], me_out)))
    sent += copies
    for c in copies:
        c.wait_recv()

    def flipped(r):
        index = me_in
        for b in range(bits):
            if r >> b & 1:
                bit = lax.rem(me_in // (1 << b), 2)
                index = index + (1 - 2 * bit) * (1 << b)
        return index

    def by_far(count):
        return sorted(range(count), key=lambda r: (-bin(r).count("1"), r))

    peers = [flipped(1 << b) for b in range(bits)]
    order = by_far(n_in // 2)
    way = [list(range(1, bits)), list(range(bits - 1, 0, -1))]
    piece = block // 2
    pending = {}
    used = {}

    def landing(h, w, stage, target):
        if stage == rounds - 1:
            return final.at[h, pl.ds(w * piece, piece), :]
        return stages.at[h, w, (n_in // 2) - (n_in >> (stage + 1)) + target]

    def send_piece(h, w, stage, index, src):
        remaining = sorted(way[w][stage:])
        b = way[w][stage]
        at = remaining.index(b)
        if index >> at & 1:
            target = (index >> (at + 1) << at) | (index & ((1 << at) - 1))
            k = used.get((h, w), 0)
            used[h, w] = k + 1
            copy = remote(
                src, landing(h, w, stage, target), sw.at[h, w, k], rw.at[h, w, k], (peers[b], me_out)
            )
            pending[h, w, stage, target] = copy
            sent.append(copy)

    def product(h, r):
        start = pl.multiple_of(flipped(r) * block, block)
        return dot(basis[h * half : (h + 1) * half, :], ebuf[:, pl.ds(start, block)]).T

    def others(h):
        for r in order:
            part[h, r] = product(h, 2 * r + 1)
            copy = remote(part.at[h, r], first.at[h, r], sc.at[h, r], rc.at[h, r], (peers[0], me_out))
            pending[h, r] = copy
            sent.append(copy)

    def own(h):
        for r in order:
            value = product(h, 2 * r)
            pending[h, r].wait_recv()
            first[h, r] = first[h, r] + value
            for w in (0, 1):
                send_piece(h, w, 0, r, first.at[h, r, pl.ds(w * piece, piece), :])

    def fold(h, stage):
        for w in (0, 1):
            remaining = sorted(way[w][stage:])
            at = remaining.index(way[w][stage])
            for target in by_far(1 << (len(remaining) - 1)):
                index = (target >> at << (at + 1)) | (target & ((1 << at) - 1))
                pending[h, w, stage, target].wait_recv()
                if stage == 0:
                    kept = first[h, index, w * piece : (w + 1) * piece, :]
                else:
                    kept = landing(h, w, stage - 1, index)[...]
                here = landing(h, w, stage, target)
                here[...] = here[...] + kept
                if stage + 1 < rounds:
                    send_piece(h, w, stage + 1, target, here)

    def spread(h):
        for d in range(1, n_out):
            theirs = pl.ds(pl.multiple_of(out_peers[d] * out_block, out_block), out_block)
            copy = remote(
                final.at[h, theirs, :], last.at[h, me_out], sz.at[h, d], rz.at[h, d], (me_in, out_peers[d])
            )
            pending[h, "z", d] = copy
            sent.append(copy)
        here = pl.ds(pl.multiple_of(me_out * out_block, out_block), out_block)
        last[h, me_out] = final[h, here, :]

    def finish(h):
        for d in range(1, n_out):
            pending[h, "z", d].wait_recv()
        total = last[h, 0]
        for d in range(1, n_out):
            total = total + last[h, d]
        out_ref[:, h * half : (h + 1) * half] = total

    def make_basis(h, left, depth):
        for c in range(0, rows, 512):
            basis[h * half : (h + 1) * half, c : c + 512] = dot(
                left, st[:depth, c : c + 512], HIGHEST
            ).astype(jnp.bfloat16)

    def store_at(at):
        def store(base, value):
            m[at + base : at + base + 8, at : at + half] = value
        return store

    sweep(whole[:half, :half], store_at(0))
    upper = m[:half, :half]
    make_basis(0, upper, half)
    others(0)
    own(0)
    x = dot(m[:half, :half], whole[:half, half:], HIGHEST)
    sweep(whole[half:, half:] - dot(x.T, x, HIGHEST), store_at(half))
    fold(0, 0)
    y = dot(x.T, m[:half, :half], HIGHEST)
    m[half:, :half] = -dot(m[half:, half:], y, HIGHEST)
    make_basis(1, m[half:, :], rank)
    others(1)
    for stage in range(1, rounds):
        fold(0, stage)
    spread(0)
    own(1)
    for stage in range(rounds):
        fold(1, stage)
    spread(1)
    finish(0)
    finish(1)
    for c in sent:
        c.wait_send()


def local(n_in, n_out, embedding, test_matrix):
    rows, width = embedding.shape
    rank = test_matrix.shape[1]
    half = rank // 2
    block = width // n_in
    share = rank // n_in
    dma = pltpu.SemaphoreType.DMA
    f32 = jnp.float32
    return pl.pallas_call(
        functools.partial(kernel, n_in, n_out),
        out_shape=jax.ShapeDtypeStruct((block // n_out, rank), f32),
        in_specs=[pl.BlockSpec(memory_space=pl.ANY)] * 2,
        out_specs=pl.BlockSpec(memory_space=pltpu.VMEM),
        scratch_shapes=[
            pltpu.VMEM((rows, width), jnp.bfloat16),
            pltpu.VMEM((width, rank), jnp.bfloat16),
            pltpu.VMEM((CHUNK, rank), f32),
            pltpu.VMEM((rank, rows), f32),
            pltpu.VMEM((rank, rows), jnp.bfloat16),
            pltpu.VMEM((rank, rank), f32),
            pltpu.VMEM((rank, rank), f32),
            pltpu.VMEM((n_in, share, rank), f32),
            pltpu.VMEM((n_out, share, rank), f32),
            pltpu.VMEM((rank, rank), f32),
            pltpu.VMEM((2, n_in // 2, block, half), f32),
            pltpu.VMEM((2, n_in // 2, block, half), f32),
            pltpu.VMEM((2, 2, n_in // 2 - 1, block // 2, half), f32),
            pltpu.VMEM((2, block, half), f32),
            pltpu.VMEM((2, n_out, block // n_out, half), f32),
            dma((rows // CHUNK,)), dma,
            dma((n_in,)), dma((n_in,)), dma((n_out,)), dma((n_out,)), dma((n_in,)), dma((n_in,)),
            dma((2, n_in // 2)), dma((2, n_in // 2)),
            dma((2, 2, n_in // 2)), dma((2, 2, n_in // 2)),
            dma((2, n_out)), dma((2, n_out)),
        ],
        compiler_params=pltpu.CompilerParams(
            collective_id=0, has_side_effects=True, vmem_limit_bytes=VMEM_LIMIT,
        ),
        cost_estimate=pl.CostEstimate(
            flops=4 * rows * width * rank, bytes_accessed=rows * width * 2, transcendentals=0
        ),
    )(embedding, test_matrix)


def solution(mesh):
    n_in, n_out = mesh.shape["inner"], mesh.shape["outer"]
    return jax.shard_map(
        functools.partial(local, n_in, n_out),
        mesh=mesh,
        in_specs=(P(("inner", "outer"), None), P()),
        out_specs=P(("inner", "outer"), None),
        check_vma=False,
    )
```

time: 287 us -> 79.2 us (0.28)
  waiting for transfers between devices: 168 us -> 0 us
  Pallas kernels: 0 us -> 77.4 us
  other arithmetic: 54.7 us -> 0 us
  matrix products: 39.2 us -> 0 us
  between operations: 14.4 us -> 0.01 us
  local copies, waits for them, and re-layouts: 9.71 us -> 1.57 us
    psum x2 -> x0, waiting for transfers between devices: 93.2 us -> none  [the longest x1 56.3 us: local(): partial_gram = lax.psum(local_gram, 'inner')]
    pallas_call x0 -> x1, Pallas kernels: none -> 77.4 us  [local(): pl.pallas_call(functools.partial(kernel, n_in, n_out), out_shape=jax.Shap...]
    reduce_scatter x2 -> x0, waiting for transfers between devices: 75 us -> none  [the longest x1 51.2 us: local(): lax.psum_scatter(lax.dot_general(embedding, basis, (((0,), (0,)), ((), ()...]
    another operation x9 -> x0, other arithmetic: 53.7 us -> none  [the longest x6 34 us: local(): lower = jnp.linalg.cholesky(gram)]
    dot_general x3 -> x0, matrix products: 31.4 us -> none  [the longest x1 13.5 us: local(): lax.dot_general(embedding, basis, (((0,), (0,)), ((), ())), preferred_ele...]
    another operation x5 -> x0, matrix products: 7.75 us -> none  [the longest x3 7.27 us: local(): lax.linalg.triangular_solve(lower, sketch, left_side=False, lower=True, t...]
    another operation x9 -> x0, local copies, waits for them, and re-layouts: 3.72 us -> none
  transfers between devices with their start and end apart: 4 -> 0, of which waited for: 4 -> 0; matrix products, arithmetic and copies ran while one was open for 0% -> 0% of each run, Pallas kernels for 0% -> 0%
where the time goes in v2:
time: 79.2 us; the launch traced here: 79 us
  Pallas kernels  77.4 us (98%)
  local copies, waits for them, and re-layouts  1.57 us (2%)
    pallas_call x1, Pallas kernels, local(): pl.pallas_call(functools.partial(kernel, n_in, n_out), out_shape=jax.Shap...  77.4 us

profile of v2, /device:TPU:0, one launch (start us, length us, event | category | flops | bytes accessed | tf_op | source)
XLA Modules:
  0.0 79.0 jit_solution(8968567132507234779)
XLA Ops:
  0.0 77.4 %shard_map.28 = f32[128,256]{1,0:T(8,128)} custom-call(bf16[3072,4096]{1,0:T(8,128)(2,1)} %e_ref.1, bf16[4096,256]{1,0:T(8,128)(2,1)} %t_ref.1), custom_call_target="tpu_custom_call" | custom-call | flops 12884901888 | bytes 25165824 | tf_op jit(solution)/shard_map/pallas_call | solution.py:298
  77.5 1.6 %copy.4 = f32[128,256]{1,0:T(8,128)} copy(f32[128,256]{1,0:T(8,128)} %shard_map.28) | data formatting | bytes 262144

commit v3 on v2

--- a/solution.py
+++ b/solution.py
@@ -65,17 +65,19 @@
                 x = x - c[k] * scaled[k]
             for at, i in enumerate(those):
                 t[i] = x[at]
+        yield
 
 
 def kernel(
     n_in, n_out, e_ref, t_ref, out_ref,
-    ebuf, tbuf, s_last, st, basis, acc, whole, recv1, recv2, m,
+    ebuf, tbuf, left1, left2, right1, right2, st, basis, acc1, acc2, m,
+    recv1_a, recv2_a, whole_a, recv1_b, recv2_b, whole_b,
     part, first, stages, final, last,
     esem, tsem, s1, r1, s2, r2, s3, r3, sc, rc, sw, rw, sz, rz,
 ):
     me_in, me_out = lax.axis_index("inner"), lax.axis_index("outer")
     rows, width = ebuf.shape
-    rank = acc.shape[0]
+    rank = acc1.shape[0]
     half = rank // 2
     bits = n_in.bit_length() - 1
     rounds = bits - 1
@@ -105,60 +107,115 @@
         span = pl.ds(pl.multiple_of(i * CHUNK, CHUNK), CHUNK)
         return dot(ebuf[span, :], tbuf[...])
 
+    def split(value):
+        high = value.astype(jnp.bfloat16)
+        rest = value - high.astype(jnp.float32)
+        middle = rest.astype(jnp.bfloat16)
+        return high, middle, (rest - middle.astype(jnp.float32)).astype(jnp.bfloat16)
+
     def keep(i, s):
         span = pl.ds(pl.multiple_of(i * CHUNK, CHUNK), CHUNK)
-        s_last[...] = s
-        st[:, span] = s.T
-
-    def gram_term(i):
-        span = pl.ds(pl.multiple_of(i * CHUNK, CHUNK), CHUNK)
-        return dot(st[:, span], s_last[...], HIGHEST)
+        t = s.T
+        st[:, span] = t
+        high, middle, low = split(s)
+        right1[:CHUNK, :] = high
+        right1[CHUNK:, :] = middle
+        right2[:CHUNK, :] = middle
+        right2[CHUNK:, :] = low
+        high, middle, low = split(t)
+        left1[:, :CHUNK] = high
+        left1[:, CHUNK:] = middle
+        left2[:, :CHUNK] = high
+        left2[:, CHUNK:] = high
+
+    def gram_term():
+        acc1[...] += dot(left1[...], right1[...])
+        acc2[...] += dot(left2[...], right2[...])
 
     test_copy.wait()
     load(0).wait()
     keep(0, sketch(0))
-    acc[...] = jnp.zeros_like(acc)
+    acc1[...] = jnp.zeros_like(acc1)
+    acc2[...] = jnp.zeros_like(acc2)
 
     def body(i, carry):
         load(i).wait()
         s = sketch(i)
-        acc[...] += gram_term(i - 1)
+        gram_term()
         keep(i, s)
         return carry
 
     lax.fori_loop(1, steps, body, 0)
-    acc[...] += gram_term(steps - 1)
-
-    share = rank // n_in
-    pl.semaphore_wait(barrier, n_in + n_out - 2)
+    gram_term()
+    acc1[...] = acc1[...] + acc2[...] + acc2[...].T
+
+    share = half // n_in
     mine = pl.ds(pl.multiple_of(me_in * share, share), share)
     sent = []
-    copies = []
-    for d in range(1, n_in):
-        theirs = pl.ds(pl.multiple_of(in_peers[d] * share, share), share)
-        copies.append(remote(acc.at[theirs, :], recv1.at[d], s1.at[d], r1.at[d], (in_peers[d], me_out)))
-    sent += copies
-    total = acc[mine, :]
-    for d in range(1, n_in):
-        copies[d - 1].wait_recv()
-        total = total + recv1[d]
-    recv2[me_out] = total
-    copies = []
-    for d in range(1, n_out):
-        copies.append(remote(recv2.at[me_out], recv2.at[me_out], s2.at[d], r2.at[d], (me_in, out_peers[d])))
-    sent += copies
-    for c in copies:
-        c.wait_recv()
-    total = recv2[0]
-    for d in range(1, n_out):
-        total = total + recv2[d]
-    whole[mine, :] = total
-    copies = []
-    for d in range(1, n_in):
-        copies.append(remote(whole.at[mine, :], whole.at[mine, :], s3.at[d], r3.at[d], (in_peers[d], me_out)))
-    sent += copies
-    for c in copies:
-        c.wait_recv()
+
+    class Sum:
+        def __init__(self, at, row, lanes, recv1, recv2, whole):
+            self.at, self.row, self.lanes = at, row, lanes
+            self.recv1, self.recv2, self.whole = recv1, recv2, whole
+
+        def rows_of(self, peer):
+            start = pl.multiple_of(self.row + peer * share, share)
+            return acc1.at[pl.ds(start, share), pl.ds(0, self.lanes)]
+
+        def start(self):
+            self.copies = [
+                remote(
+                    self.rows_of(in_peers[d]), self.recv1.at[d],
+                    s1.at[self.at, d], r1.at[self.at, d], (in_peers[d], me_out),
+                )
+                for d in range(1, n_in)
+            ]
+            sent.extend(self.copies)
+
+        def exchange(self):
+            total = self.rows_of(me_in)[...]
+            for d in range(1, n_in):
+                self.copies[d - 1].wait_recv()
+                total = total + self.recv1[d]
+            self.recv2[me_out] = total
+            self.copies = [
+                remote(
+                    self.recv2.at[me_out], self.recv2.at[me_out],
+                    s2.at[self.at, d], r2.at[self.at, d], (me_in, out_peers[d]),
+                )
+                for d in range(1, n_out)
+            ]
+            sent.extend(self.copies)
+
+        def gather(self):
+            for c in self.copies:
+                c.wait_recv()
+            total = self.recv2[0]
+            for d in range(1, n_out):
+                total = total + self.recv2[d]
+            self.whole[mine, :] = total
+            self.copies = [
+                remote(
+                    self.whole.at[mine, :], self.whole.at[mine, :],
+                    s3.at[self.at, d], r3.at[self.at, d], (in_peers[d], me_out),
+                )
+                for d in range(1, n_in)
+            ]
+            sent.extend(self.copies)
+
+        def done(self):
+            for c in self.copies:
+                c.wait_recv()
+
+    sum_a = Sum(0, 0, half, recv1_a, recv2_a, whole_a)
+    sum_b = Sum(1, half, rank, recv1_b, recv2_b, whole_b)
+    pl.semaphore_wait(barrier, n_in + n_out - 2)
+    sum_a.start()
+    sum_b.start()
+    sum_a.exchange()
+    sum_b.exchange()
+    sum_a.gather()
+    sum_a.done()
 
     def flipped(r):
         index = me_in
@@ -201,26 +258,28 @@
         start = pl.multiple_of(flipped(r) * block, block)
         return dot(basis[h * half : (h + 1) * half, :], ebuf[:, pl.ds(start, block)]).T
 
-    def others(h):
+    def others(h, beside):
         for r in order:
             part[h, r] = product(h, 2 * r + 1)
+            beside()
             copy = remote(part.at[h, r], first.at[h, r], sc.at[h, r], rc.at[h, r], (peers[0], me_out))
             pending[h, r] = copy
             sent.append(copy)
 
-    def own(h):
+    def own(h, beside):
         for r in order:
             value = product(h, 2 * r)
+            beside()
             pending[h, r].wait_recv()
             first[h, r] = first[h, r] + value
             for w in (0, 1):
                 send_piece(h, w, 0, r, first.at[h, r, pl.ds(w * piece, piece), :])
 
     def fold(h, stage):
-        for w in (0, 1):
-            remaining = sorted(way[w][stage:])
-            at = remaining.index(way[w][stage])
-            for target in by_far(1 << (len(remaining) - 1)):
+        count = 1 << (len(way[0][stage:]) - 1)
+        for target in by_far(count):
+            for w in (0, 1):
+                at = sorted(way[w][stage:]).index(way[w][stage])
                 index = (target >> at << (at + 1)) | (target & ((1 << at) - 1))
                 pending[h, w, stage, target].wait_recv()
                 if stage == 0:
@@ -262,22 +321,35 @@
             m[at + base : at + base + 8, at : at + half] = value
         return store
 
-    sweep(whole[:half, :half], store_at(0))
-    upper = m[:half, :half]
-    make_basis(0, upper, half)
-    others(0)
-    own(0)
-    x = dot(m[:half, :half], whole[:half, half:], HIGHEST)
-    sweep(whole[half:, half:] - dot(x.T, x, HIGHEST), store_at(half))
+    panels = half // 8
+    for panel, _ in enumerate(sweep(whole_a[...], store_at(0))):
+        if panel == panels // 2:
+            sum_b.gather()
+    make_basis(0, m[:half, :half], half)
+    sum_b.done()
+    x = dot(m[:half, :half], whole_b[:, :half].T, HIGHEST)
+    second = sweep(whole_b[:, half:] - dot(x.T, x, HIGHEST), store_at(half))
+
+    def advance():
+        for _ in range(panels // n_in):
+            next(second, None)
+
+    def nothing():
+        pass
+
+    others(0, advance)
+    own(0, advance)
+    for _ in second:
+        pass
     fold(0, 0)
     y = dot(x.T, m[:half, :half], HIGHEST)
     m[half:, :half] = -dot(m[half:, half:], y, HIGHEST)
     make_basis(1, m[half:, :], rank)
-    others(1)
+    others(1, nothing)
     for stage in range(1, rounds):
         fold(0, stage)
     spread(0)
-    own(1)
+    own(1, nothing)
     for stage in range(rounds):
         fold(1, stage)
     spread(1)
@@ -292,7 +364,7 @@
     rank = test_matrix.shape[1]
     half = rank // 2
     block = width // n_in
-    share = rank // n_in
+    share = half // n_in
     dma = pltpu.SemaphoreType.DMA
     f32 = jnp.float32
     return pl.pallas_call(
@@ -303,21 +375,28 @@
         scratch_shapes=[
             pltpu.VMEM((rows, width), jnp.bfloat16),
             pltpu.VMEM((width, rank), jnp.bfloat16),
-            pltpu.VMEM((CHUNK, rank), f32),
+            pltpu.VMEM((rank, 2 * CHUNK), jnp.bfloat16),
+            pltpu.VMEM((rank, 2 * CHUNK), jnp.bfloat16),
+            pltpu.VMEM((2 * CHUNK, rank), jnp.bfloat16),
+            pltpu.VMEM((2 * CHUNK, rank), jnp.bfloat16),
             pltpu.VMEM((rank, rows), f32),
             pltpu.VMEM((rank, rows), jnp.bfloat16),
             pltpu.VMEM((rank, rank), f32),
             pltpu.VMEM((rank, rank), f32),
+            pltpu.VMEM((rank, rank), f32),
+            pltpu.VMEM((n_in, share, half), f32),
+            pltpu.VMEM((n_out, share, half), f32),
+            pltpu.VMEM((half, half), f32),
             pltpu.VMEM((n_in, share, rank), f32),
             pltpu.VMEM((n_out, share, rank), f32),
-            pltpu.VMEM((rank, rank), f32),
+            pltpu.VMEM((half, rank), f32),
             pltpu.VMEM((2, n_in // 2, block, half), f32),
             pltpu.VMEM((2, n_in // 2, block, half), f32),
             pltpu.VMEM((2, 2, n_in // 2 - 1, block // 2, half), f32),
             pltpu.VMEM((2, block, half), f32),
             pltpu.VMEM((2, n_out, block // n_out, half), f32),
             dma((rows // CHUNK,)), dma,
-            dma((n_in,)), dma((n_in,)), dma((n_out,)), dma((n_out,)), dma((n_in,)), dma((n_in,)),
+            dma((2, n_in)), dma((2, n_in)), dma((2, n_out)), dma((2, n_out)), dma((2, n_in)), dma((2, n_in)),
             dma((2, n_in // 2)), dma((2, n_in // 2)),
             dma((2, 2, n_in // 2)), dma((2, 2, n_in // 2)),
             dma((2, n_out)), dma((2, n_out)),

time: 79.2 us -> 75 us (0.947)
  Pallas kernels: 77.4 us -> 73.2 us
    pallas_call x1, Pallas kernels: 77.4 us -> 73.2 us  [local(): pl.pallas_call(functools.partial(kernel, n_in, n_out), out_shape=jax.Shap...]
where the time goes in v3:
time: 75 us; the launch traced here: 74.8 us
  Pallas kernels  73.2 us (98%)
  local copies, waits for them, and re-layouts  1.57 us (2%)
    pallas_call x1, Pallas kernels, local(): pl.pallas_call(functools.partial(kernel, n_in, n_out), out_shape=jax.Shap...  73.2 us
    unnamed x1, local copies, waits for them, and re-layouts  1.57 us

profile of v3, /device:TPU:0, one launch (start us, length us, event | category | flops | bytes accessed | tf_op | source)
XLA Modules:
  0.0 74.8 jit_solution(7811893238153500318)
XLA Ops:
  0.0 73.2 %shard_map.28 = f32[128,256]{1,0:T(8,128)} custom-call(bf16[3072,4096]{1,0:T(8,128)(2,1)} %e_ref.1, bf16[4096,256]{1,0:T(8,128)(2,1)} %t_ref.1), custom_call_target="tpu_custom_call" | custom-call | flops 12884901888 | bytes 25165824 | tf_op jit(solution)/shard_map/pallas_call | solution.py:370
  73.3 1.6 %copy.4 = f32[128,256]{1,0:T(8,128)} copy(f32[128,256]{1,0:T(8,128)} %shard_map.28) | data formatting | bytes 262144

commit v4 on v3

--- a/solution.py
+++ b/solution.py
@@ -10,7 +10,8 @@
 MESH = pl.DeviceIdType.MESH
 HIGHEST = lax.Precision.HIGHEST
 VMEM_LIMIT = 58 * 1024 * 1024
-CHUNK = 384
+CHUNK = 256
+AHEAD = 4
 
 
 def dot(a, b, precision=None):
@@ -100,7 +101,7 @@
         span = pl.ds(pl.multiple_of(i * CHUNK, CHUNK), CHUNK)
         return pltpu.make_async_copy(e_ref.at[span, :], ebuf.at[span, :], esem.at[i])
 
-    for i in range(steps):
+    for i in range(AHEAD):
         load(i).start()
 
     def sketch(i):
@@ -134,12 +135,18 @@
 
     test_copy.wait()
     load(0).wait()
+    load(AHEAD).start()
     keep(0, sketch(0))
     acc1[...] = jnp.zeros_like(acc1)
     acc2[...] = jnp.zeros_like(acc2)
 
     def body(i, carry):
         load(i).wait()
+
+        @pl.when(i + AHEAD < steps)
+        def _():
+            load(i + AHEAD).start()
+
         s = sketch(i)
         gram_term()
         keep(i, s)
@@ -230,14 +237,19 @@
 
     peers = [flipped(1 << b) for b in range(bits)]
     order = by_far(n_in // 2)
-    way = [list(range(1, bits)), list(range(bits - 1, 0, -1))]
-    piece = block // 2
+    up, down = list(range(1, bits)), list(range(bits - 1, 0, -1))
+    way = [up if d % 2 else down for d in range(n_out)]
+    turns = list(range(1, n_out)) + [0]
+
+    def rows_for(d):
+        return pl.ds(pl.multiple_of(out_peers[d] * out_block, out_block), out_block)
+
     pending = {}
     used = {}
 
     def landing(h, w, stage, target):
         if stage == rounds - 1:
-            return final.at[h, pl.ds(w * piece, piece), :]
+            return final.at[h, w]
         return stages.at[h, w, (n_in // 2) - (n_in >> (stage + 1)) + target]
 
     def send_piece(h, w, stage, index, src):
@@ -258,49 +270,44 @@
         start = pl.multiple_of(flipped(r) * block, block)
         return dot(basis[h * half : (h + 1) * half, :], ebuf[:, pl.ds(start, block)]).T
 
-    def others(h, beside):
+    def others(h):
         for r in order:
             part[h, r] = product(h, 2 * r + 1)
-            beside()
             copy = remote(part.at[h, r], first.at[h, r], sc.at[h, r], rc.at[h, r], (peers[0], me_out))
             pending[h, r] = copy
             sent.append(copy)
 
-    def own(h, beside):
+    def own(h):
         for r in order:
             value = product(h, 2 * r)
-            beside()
             pending[h, r].wait_recv()
             first[h, r] = first[h, r] + value
-            for w in (0, 1):
-                send_piece(h, w, 0, r, first.at[h, r, pl.ds(w * piece, piece), :])
+            for w in turns:
+                send_piece(h, w, 0, r, first.at[h, r, rows_for(w), :])
 
     def fold(h, stage):
         count = 1 << (len(way[0][stage:]) - 1)
         for target in by_far(count):
-            for w in (0, 1):
+            for w in turns:
                 at = sorted(way[w][stage:]).index(way[w][stage])
                 index = (target >> at << (at + 1)) | (target & ((1 << at) - 1))
                 pending[h, w, stage, target].wait_recv()
                 if stage == 0:
-                    kept = first[h, index, w * piece : (w + 1) * piece, :]
+                    kept = first[h, index, rows_for(w), :]
                 else:
                     kept = landing(h, w, stage - 1, index)[...]
                 here = landing(h, w, stage, target)
                 here[...] = here[...] + kept
                 if stage + 1 < rounds:
                     send_piece(h, w, stage + 1, target, here)
-
-    def spread(h):
-        for d in range(1, n_out):
-            theirs = pl.ds(pl.multiple_of(out_peers[d] * out_block, out_block), out_block)
-            copy = remote(
-                final.at[h, theirs, :], last.at[h, me_out], sz.at[h, d], rz.at[h, d], (me_in, out_peers[d])
-            )
-            pending[h, "z", d] = copy
-            sent.append(copy)
-        here = pl.ds(pl.multiple_of(me_out * out_block, out_block), out_block)
-        last[h, me_out] = final[h, here, :]
+                elif w:
+                    copy = remote(
+                        here, last.at[h, me_out], sz.at[h, w], rz.at[h, w], (me_in, out_peers[w])
+                    )
+                    pending[h, "z", w] = copy
+                    sent.append(copy)
+                else:
+                    last[h, me_out] = here[...]
 
     def finish(h):
         for d in range(1, n_out):
@@ -326,33 +333,24 @@
         if panel == panels // 2:
             sum_b.gather()
     make_basis(0, m[:half, :half], half)
+    others(0)
+    own(0)
     sum_b.done()
     x = dot(m[:half, :half], whole_b[:, :half].T, HIGHEST)
     second = sweep(whole_b[:, half:] - dot(x.T, x, HIGHEST), store_at(half))
 
-    def advance():
-        for _ in range(panels // n_in):
-            next(second, None)
-
-    def nothing():
-        pass
-
-    others(0, advance)
-    own(0, advance)
-    for _ in second:
-        pass
-    fold(0, 0)
+    for panel, _ in enumerate(second):
+        if panel == 5 * panels // 8:
+            fold(0, 0)
     y = dot(x.T, m[:half, :half], HIGHEST)
     m[half:, :half] = -dot(m[half:, half:], y, HIGHEST)
     make_basis(1, m[half:, :], rank)
-    others(1, nothing)
     for stage in range(1, rounds):
         fold(0, stage)
-    spread(0)
-    own(1, nothing)
+    others(1)
+    own(1)
     for stage in range(rounds):
         fold(1, stage)
-    spread(1)
     finish(0)
     finish(1)
     for c in sent:
@@ -392,13 +390,13 @@
             pltpu.VMEM((half, rank), f32),
             pltpu.VMEM((2, n_in // 2, block, half), f32),
             pltpu.VMEM((2, n_in // 2, block, half), f32),
-            pltpu.VMEM((2, 2, n_in // 2 - 1, block // 2, half), f32),
-            pltpu.VMEM((2, block, half), f32),
+            pltpu.VMEM((2, n_out, n_in // 2 - 1, block // n_out, half), f32),
+            pltpu.VMEM((2, n_out, block // n_out, half), f32),
             pltpu.VMEM((2, n_out, block // n_out, half), f32),
             dma((rows // CHUNK,)), dma,
             dma((2, n_in)), dma((2, n_in)), dma((2, n_out)), dma((2, n_out)), dma((2, n_in)), dma((2, n_in)),
             dma((2, n_in // 2)), dma((2, n_in // 2)),
-            dma((2, 2, n_in // 2)), dma((2, 2, n_in // 2)),
+            dma((2, n_out, n_in // 2)), dma((2, n_out, n_in // 2)),
             dma((2, n_out)), dma((2, n_out)),
         ],
         compiler_params=pltpu.CompilerParams(

time: 75 us -> 69.6 us (0.928)
  Pallas kernels: 73.2 us -> 67.9 us
    pallas_call x1, Pallas kernels: 73.2 us -> 67.9 us  [local(): pl.pallas_call(functools.partial(kernel, n_in, n_out), out_shape=jax.Shap...]
where the time goes in v4:
time: 69.6 us; the launch traced here: 69.5 us
  Pallas kernels  67.9 us (98%)
  local copies, waits for them, and re-layouts  1.57 us (2%)
    pallas_call x1, Pallas kernels, local(): pl.pallas_call(functools.partial(kernel, n_in, n_out), out_shape=jax.Shap...  67.9 us
    unnamed x1, local copies, waits for them, and re-layouts  1.57 us

profile of v4, /device:TPU:0, one launch (start us, length us, event | category | flops | bytes accessed | tf_op | source)
XLA Modules:
  0.0 69.5 jit_solution(9191210998350218723)
XLA Ops:
  0.0 67.9 %shard_map.28 = f32[128,256]{1,0:T(8,128)} custom-call(bf16[3072,4096]{1,0:T(8,128)(2,1)} %e_ref.1, bf16[4096,256]{1,0:T(8,128)(2,1)} %t_ref.1), custom_call_target="tpu_custom_call" | custom-call | flops 12884901888 | bytes 25165824 | tf_op jit(solution)/shard_map/pallas_call | solution.py:368
  67.9 1.6 %copy.4 = f32[128,256]{1,0:T(8,128)} copy(f32[128,256]{1,0:T(8,128)} %shard_map.28) | data formatting | bytes 262144

commit v5 on v4

--- a/solution.py
+++ b/solution.py
@@ -270,20 +270,25 @@
         start = pl.multiple_of(flipped(r) * block, block)
         return dot(basis[h * half : (h + 1) * half, :], ebuf[:, pl.ds(start, block)]).T
 
-    def others(h):
-        for r in order:
-            part[h, r] = product(h, 2 * r + 1)
-            copy = remote(part.at[h, r], first.at[h, r], sc.at[h, r], rc.at[h, r], (peers[0], me_out))
-            pending[h, r] = copy
-            sent.append(copy)
-
-    def own(h):
-        for r in order:
-            value = product(h, 2 * r)
-            pending[h, r].wait_recv()
-            first[h, r] = first[h, r] + value
-            for w in turns:
-                send_piece(h, w, 0, r, first.at[h, r, rows_for(w), :])
+    def give(h, r):
+        part[h, r] = product(h, 2 * r + 1)
+        copy = remote(part.at[h, r], first.at[h, r], sc.at[h, r], rc.at[h, r], (peers[0], me_out))
+        pending[h, r] = copy
+        sent.append(copy)
+
+    def take(h, r):
+        value = product(h, 2 * r)
+        pending[h, r].wait_recv()
+        first[h, r] = first[h, r] + value
+        for w in turns:
+            send_piece(h, w, 0, r, first.at[h, r, rows_for(w), :])
+
+    def products(h):
+        give(h, order[0])
+        for before, r in zip(order, order[1:]):
+            give(h, r)
+            take(h, before)
+        take(h, order[-1])
 
     def fold(h, stage):
         count = 1 << (len(way[0][stage:]) - 1)
@@ -333,22 +338,20 @@
         if panel == panels // 2:
             sum_b.gather()
     make_basis(0, m[:half, :half], half)
-    others(0)
-    own(0)
+    products(0)
     sum_b.done()
     x = dot(m[:half, :half], whole_b[:, :half].T, HIGHEST)
+    y = dot(x.T, m[:half, :half], HIGHEST)
     second = sweep(whole_b[:, half:] - dot(x.T, x, HIGHEST), store_at(half))
 
     for panel, _ in enumerate(second):
-        if panel == 5 * panels // 8:
+        if panel == panels // 2:
             fold(0, 0)
-    y = dot(x.T, m[:half, :half], HIGHEST)
     m[half:, :half] = -dot(m[half:, half:], y, HIGHEST)
     make_basis(1, m[half:, :], rank)
     for stage in range(1, rounds):
         fold(0, stage)
-    others(1)
-    own(1)
+    products(1)
     for stage in range(rounds):
         fold(1, stage)
     finish(0)

time: 69.6 us -> 68.5 us (0.984)
  Pallas kernels: 67.9 us -> 66.8 us
    pallas_call x1, Pallas kernels: 67.9 us -> 66.8 us  [local(): pl.pallas_call(functools.partial(kernel, n_in, n_out), out_shape=jax.Shap...]
where the time goes in v5:
time: 68.5 us; the launch traced here: 68.4 us
  Pallas kernels  66.8 us (98%)
  local copies, waits for them, and re-layouts  1.57 us (2%)
    pallas_call x1, Pallas kernels, local(): pl.pallas_call(functools.partial(kernel, n_in, n_out), out_shape=jax.Shap...  66.8 us
    unnamed x1, local copies, waits for them, and re-layouts  1.57 us

profile of v5, /device:TPU:0, one launch (start us, length us, event | category | flops | bytes accessed | tf_op | source)
XLA Modules:
  0.0 68.4 jit_solution(17203200158127247621)
XLA Ops:
  0.0 66.8 %shard_map.28 = f32[128,256]{1,0:T(8,128)} custom-call(bf16[3072,4096]{1,0:T(8,128)(2,1)} %e_ref.1, bf16[4096,256]{1,0:T(8,128)(2,1)} %t_ref.1), custom_call_target="tpu_custom_call" | custom-call | flops 12884901888 | bytes 25165824 | tf_op jit(solution)/shard_map/pallas_call | solution.py:371
  66.8 1.6 %copy.4 = f32[128,256]{1,0:T(8,128)} copy(f32[128,256]{1,0:T(8,128)} %shard_map.28) | data formatting | bytes 262144
